TPU v7x, 256 devices: a whole 4x4x8 slice. The times are simulated.
256 devices in a mesh: lat: 16 (over z_lo, y, core), lev: 4 (over x), ocn: 4 (over z_hi).
Axes of the slice: x: 4, y: 4, z: 8 (z_hi: 4, z_lo: 2; z = z_hi * 2 + z_lo), core: 2. Of those that a mesh axis runs over, the one named last changes fastest.
Arguments:
- atmos_fields: bfloat16 [2, 24, 2560, 5632], P(None, 'lev', ('lat', 'ocn')), may hold values from -6 to 6
- lat_points: int32 [2560], P(('lat', 'ocn')), may hold values from 20 to 5632, as said below
- wave_order: int32 [256], replicated, may hold values from 0 to 255, each once
- legendre: bfloat16 [256, 2560, 1536], P(('lat', 'ocn'), None, 'lev'), may hold values from -0.125 to 0.125
- column_weight: bfloat16 [2, 24], P(None, 'lev'), may hold values from -1.25 to 1.25
- block_remap: int32 [2560, 44], P(('lat', 'ocn'), 'lev'), may hold values from 0 to 17407, as said below
- ocean_temp: float32 [1024, 2176], P(('lat', 'ocn')), may hold values from -6 to 6
- ocean_salt: float32 [1024, 2176], P(('lat', 'ocn')), may hold values from -6 to 6
- sea_mask: int32 [1024, 17], P(('lat', 'ocn')), may hold values 0 or 1
Outputs:
- spectra: float32 [256, 96, 1536], P(('lat', 'ocn'), None, 'lev')
- temp_next: float32 [1024, 2176], P(('lat', 'ocn'))
- salt_next: float32 [1024, 2176], P(('lat', 'ocn'))
- surface_temp: float32 [2560, 5632], P(('lat', 'ocn'), 'lev')
Inputs may be any that keep to these rules, and one draw needn't show every extreme that they name: `lat_points`: a multiple of 4 for every latitude row. `wave_order`: each wavenumber appears once. `block_remap`: the blocks of latitude band g (rows g * 40 onward) name tiles of ocean sections g - 1, g or g + 1 only; section g holds tiles g * 16 * 17 onward, in row order.
All inputs are finite; a program needn't handle non-finite values. No bound on the sum of `sea_mask` on one device may be relied on, other than what follows from the above.
Results may differ from a plain program's by a relative error of at most 0.0037.
Values may be sent and summed in bfloat16 or wider, within the bound.
A program may use at most 128 MiB of HBM per device.

v0:
```python
import math
import jax
import jax.numpy as jnp
from jax import lax
from jax.sharding import PartitionSpec as P

FIELDS = 2
BLOCK = 128
FULL_TURN = 2.0 * math.pi
DIFFUSION = 0.2
COUPLING = 0.5


def with_halo(cells, sides, width):
    for axis, dim in sides:
        count = lax.axis_size(axis)
        ends = count - 1
        head = lax.slice_in_dim(cells, 0, width, axis=dim)
        tail = lax.slice_in_dim(cells, cells.shape[dim] - width, cells.shape[dim], axis=dim)
        cells = jnp.concatenate(
            [
                lax.ppermute(tail, axis, [(i, (i + 1) % count) for i in range(ends)]),
                cells,
                lax.ppermute(head, axis, [((i + 1) % count, i) for i in range(ends)]),
            ],
            axis=dim,
        )
    return cells


def fourier_table(wave_order, length):
    points = jnp.arange(length, dtype=jnp.int32)
    phase = wave_order[None, :] * points[:, None] % length
    angle = phase.astype(jnp.float32) * (FULL_TURN / length)
    table = jnp.concatenate([jnp.cos(angle), -jnp.sin(angle)], axis=1).astype(jnp.bfloat16)
    return (table, points)


def body(
    atmos_fields,
    lat_points,
    wave_order,
    legendre,
    column_weight,
    block_remap,
    ocean_temp,
    ocean_salt,
    sea_mask,
):
    nfields, lev_dev, lat_band, lon_count = atmos_fields.shape
    wave_count = wave_order.shape[0]
    table, points = fourier_table(wave_order, lon_count)
    point_mask = points[None, :] < lat_points[:, None]
    masked = jnp.where(point_mask[None, None], atmos_fields, jnp.zeros((), jnp.bfloat16))
    inverse_root = 1.0 / jnp.sqrt(lat_points.astype(jnp.float32))
    weights = jnp.where(
        2 * wave_order[None, :] < lat_points[:, None],
        inverse_root[:, None],
        jnp.zeros((), jnp.float32),
    )
    field_count = masked.shape[0]
    raw_sums = jnp.dot(masked.reshape(-1, lon_count), table, preferred_element_type=jnp.float32)
    raw_sums = raw_sums.reshape(field_count, lev_dev, lat_band, 2, wave_count)
    coeffs = (raw_sums * weights[None, None, :, None, :]).astype(jnp.bfloat16)
    regrouped = lax.all_to_all(
        coeffs.transpose(4, 1, 0, 3, 2).reshape(wave_count, lev_dev * field_count * 2, lat_band),
        ("lat", "ocn"),
        split_axis=0,
        concat_axis=2,
        tiled=True,
    )
    spectra = jnp.einsum(
        "srj,sjd->srd",
        lax.all_gather(regrouped, "lev", axis=1, tiled=True),
        legendre,
        preferred_element_type=jnp.float32,
    )
    ocean_rows, ocean_cols = ocean_temp.shape
    tile_count = ocean_rows * ocean_cols // BLOCK
    band_index = lax.axis_index(("lat", "ocn"))
    targets = block_remap.reshape(-1)
    local_slot = (targets // tile_count - band_index + 1) * tile_count + targets % tile_count
    partial_sum = jnp.einsum(
        "ql,qljk->qjk", column_weight, masked, preferred_element_type=jnp.float32
    )
    quarter = lon_count // lax.axis_size("lev")
    totals = lax.psum(partial_sum, "lev")
    own_flux = lax.dynamic_slice_in_dim(totals, lax.axis_index("lev") * quarter, quarter, 2)
    block_rows = (
        own_flux.reshape(FIELDS, lat_band, quarter // BLOCK, BLOCK)
        .transpose(1, 2, 0, 3)
        .reshape(-1, FIELDS * BLOCK)
    )
    outgoing = jax.ops.segment_sum(block_rows, local_slot, num_segments=3 * tile_count)
    widened = with_halo(outgoing, ((("lat", "ocn"), 0),), tile_count)
    arrived = (
        widened[:tile_count] + widened[2 * tile_count : 3 * tile_count] + widened[4 * tile_count :]
    )
    tile_sums = lax.psum(arrived, "lev")
    forcing = (
        tile_sums.reshape(ocean_rows, ocean_cols // BLOCK, FIELDS, BLOCK)
        .transpose(2, 0, 1, 3)
        .reshape(FIELDS, ocean_rows, ocean_cols)
    )
    sea_cells = (
        jnp.broadcast_to(sea_mask[:, :, None], (ocean_rows, ocean_cols // BLOCK, BLOCK))
        .reshape(ocean_rows, ocean_cols)
        .astype(jnp.float32)
    )
    ocean_state = jnp.stack([ocean_temp, ocean_salt])
    padded = with_halo(ocean_state, ((("lat", "ocn"), 1),), 1)
    laplace = (
        padded[:, 2:]
        + padded[:, :-2]
        + jnp.roll(ocean_state, 1, 2)
        + jnp.roll(ocean_state, -1, 2)
        - 4.0 * ocean_state
    )
    updated = ocean_state + DIFFUSION * laplace + COUPLING * sea_cells[None] * forcing
    temp_next = updated[0]
    salt_next = updated[1]
    returned = with_halo(temp_next, ((("lat", "ocn"), 0),), ocean_rows)
    tiles_near = returned.reshape(3 * tile_count, BLOCK)
    surface = jnp.take(tiles_near, local_slot, axis=0).reshape(lat_band, quarter)
    own_points = lax.axis_index("lev") * quarter + jnp.arange(quarter, dtype=jnp.int32)
    surface_temp = jnp.where(
        own_points[None, :] < lat_points[:, None], surface, jnp.zeros((), jnp.float32)
    )
    return (spectra, temp_next, salt_next, surface_temp)


def solution(mesh):
    placed = (
        P(None, "lev", ("lat", "ocn"), None),
        P(("lat", "ocn")),
        P(),
        P(("lat", "ocn"), None, "lev"),
        P(None, "lev"),
        P(("lat", "ocn"), "lev"),
        P(("lat", "ocn"), None),
        P(("lat", "ocn"), None),
        P(("lat", "ocn"), None),
    )
    return jax.shard_map(
        body,
        mesh=mesh,
        in_specs=placed,
        out_specs=(
            P(("lat", "ocn"), None, "lev"),
            P(("lat", "ocn"), None),
            P(("lat", "ocn"), None),
            P(("lat", "ocn"), "lev"),
        ),
        check_vma=False,
    )
```

profile of v0, /device:TPU:1, one launch (start us, length us, event | category | flops | bytes accessed | tf_op | source)
XLA Modules:
  0.0 199.3 jit_solution(3094316823144433169)
XLA Ops:
  7.2 0.0 copy-start
  7.2 0.0 all-reduce.3.cloned.1.call-start
  7.2 0.8 iota_compare_fusion
  8.1 3.6 %broadcast_select_fusion = bf16[2,6,40,5632]{3,2,1,0:T(8,128)(2,1)S(1)} fusion(bf16[2,6,40,5632]{3,2,1,0:T(8,128)(2,1)} %param.9, pred[40,5632]{1,0:T(8,128)(4,1)S(1)} %iota_compare_fusion), kind=kLoop, calls=%fused_computation.16 | loop fusion | flops 2703360 | bytes 11038720 | tf_op jit(solution)/shard_map/jit(_where)/select_n | solution.py:54
  11.7 0.0 copy-start.7
  11.7 0.0 copy-start.8
  11.7 2.4 %fusion = f32[2,1,40,5632]{3,1,2,0:T(1,128)S(1)} fusion(bf16[2,6,40,5632]{3,2,1,0:T(8,128)(2,1)S(1)} %broadcast_select_fusion, bf16[2,6,1,1]{1,0,2,3:T(2,128)(2,1)S(1)} %bitcast.59), kind=kOutput, calls=%fused_computation.3 | convolution fusion | flops 5406720 | bytes 7208984 | tf_op jit(solution)/shard_map/ql,qljk->qjk/dot_general | solution.py:83
  14.2 1.4 copy.59
  15.5 0.0 all-reduce.3.cloned.1.call-update
  15.6 0.0 slice-start
  15.6 25.0 %cosine_convert_fusion = (bf16[5632,256]{0,1:T(8,128)(2,1)S(1)}, bf16[5632,256]{0,1:T(8,128)(2,1)S(1)}) fusion(s32[256]{0:T(256)S(1)} %copy-done.8), kind=kLoop, calls=%fused_computation.9 | loop fusion | flops 17301504 | bytes 5768192 | tf_op jit(solution)/shard_map/convert
  40.6 0.0 slice-start.1
  40.7 2.9 %pad_maximum_fusion = bf16[5632,512]{0,1:T(8,128)(2,1)} fusion(bf16[5632,256]{0,1:T(8,128)(2,1)S(1)} %get-tuple-element.21, bf16[5632,256]{0,1:T(8,128)(2,1)S(1)} %get-tuple-element.20), kind=kLoop, calls=%fused_computation.7 | loop fusion | flops 11534336 | bytes 11534336 | tf_op jit(solution)/shard_map/concatenate | solution.py:35
  43.5 0.1 compare_select_fusion
  43.6 5.7 %fusion.15 = bf16[256,6,2,2,40]{0,4,3,1,2:T(8,128)(2,1)S(1)} fusion(bf16[2,256,5632,1,1]{2,1,0,4,3:T(8,128)(2,1)} %bitcast.64, bf16[2,6,40,5632]{3,2,1,0:T(8,128)(2,1)S(1)} %bitcast.61, f32[256,40]{0,1:T(8,128)S(1)} %compare_select_fusion), kind=kOutput, calls=%fused_computation.20 | convolution fusion | flops 2768732160 | bytes 11706368 | tf_op jit(solution)/shard_map/dot_general | solution.py:62
  49.3 0.0 copy-start.5
  49.4 1.0 copy.32
  50.3 3.4 %reshape.235 = bf16[64,2,1920]{2,1,0:T(2,128)(2,1)} reshape(bf16[256,24,40]{2,1,0:T(8,128)(2,1)S(1)} %copy.32) | data formatting | bytes 983040
  53.7 13.3 %all-to-all-start = ((bf16[64,2,1920]{2,1,0:T(2,128)(2,1)}), bf16[64,2,1920]{2,1,0:T(2,128)(2,1)S(1)}, u32[]{:S(2)}, u32[]{:S(2)}) async-start(bf16[64,2,1920]{2,1,0:T(2,128)(2,1)} %reshape.235), calls=%async_computation | async-start | bytes 983040 | tf_op jit(solution)/shard_map/all_to_all | solution.py:65
  67.1 0.0 all-reduce.5.cloned.1.call-start
  67.2 0.1 copy.35
  67.2 0.1 rem.47
  67.4 0.1 copy.36
  67.5 0.1 div.26
  67.6 0.1 copy.34
  67.7 0.1 ne.88
  67.9 10.6 %all-reduce.3.cloned.1.call-done = f32[2,40,5632]{2,1,0:T(8,128)} async-done(((f32[2,40,5632]{2,1,0:T(8,128)}), f32[2,40,5632]{2,1,0:T(8,128)}) %all-reduce.3.cloned.1.call-update) | async-done | bytes 1802256 | tf_op jit(solution)/shard_map/psum | solution.py:87
  78.5 1.0 constant_dynamic-slice_fusion
  79.6 0.1 reshape.208
  79.6 0.3 copy.37
  80.0 3.1 %scatter_custom_fusion = f32[816,256]{1,0:T(8,128)S(1)} fusion(s32[440]{0:T(512)S(1)} %bitcast.81, f32[55,8,2,128]{3,2,1,0:T(2,128)S(1)} %bitcast.75, f32[]{:T(128)} %constant.40.clone.1), kind=kCustom, calls=%fused_computation.35 | custom fusion | flops 112640 | bytes 1286148 | tf_op jit(solution)/shard_map/scatter-add | solution.py:94
  83.2 6.3 %collective-permute-start.3 = (f32[272,256]{1,0:T(8,128)S(1)}, f32[272,256]{1,0:T(8,128)S(1)}, u32[]{:S(2)}, u32[]{:S(2)}) collective-permute-start(f32[272,256]{1,0:T(8,128)S(1)} %get-tuple-element.9), channel_id=1, source_target_pairs={{1,0},{2,1},{3,2},{16,3},{17,16},{18,17},{19,18},{32,19},{33,32},{... | collective-permute-start | bytes 835592 | tf_op jit(solution)/shard_map/ppermute | solution.py:24
  89.5 1.9 collective-permute-start.2
  91.4 8.1 %collective-permute-done.3 = f32[272,256]{1,0:T(8,128)S(1)} collective-permute-done((f32[272,256]{1,0:T(8,128)S(1)}, f32[272,256]{1,0:T(8,128)S(1)}, u32[]{:S(2)}, u32[]{:S(2)}) %collective-permute-start.3) | collective-permute-done | bytes 278560 | tf_op jit(solution)/shard_map/ppermute | solution.py:24
  99.6 8.0 %collective-permute-done.2 = f32[272,256]{1,0:T(8,128)S(1)} collective-permute-done((f32[272,256]{1,0:T(8,128)S(1)}, f32[272,256]{1,0:T(8,128)S(1)}, u32[]{:S(2)}, u32[]{:S(2)}) %collective-permute-start.2) | collective-permute-done | bytes 278560 | tf_op jit(solution)/shard_map/ppermute | solution.py:22
  107.6 0.1 fusion.24
  107.6 0.0 copy-start.6
  107.7 0.1 reshape.210
  107.9 0.8 reshape.211
  108.6 0.0 all-reduce.5.cloned.1.call-update
  108.6 0.0 all-gather.2.cloned.1.call-start
  108.7 1.9 collective-permute-start.1
  110.7 5.8 %collective-permute-start = (f32[2,1,2176]{2,1,0:T(1,128)S(1)}, f32[2,1,2176]{2,1,0:T(1,128)S(1)}, u32[]{:S(2)}, u32[]{:S(2)}) collective-permute-start(f32[2,1,2176]{2,1,0:T(1,128)S(1)} %get-tuple-element.16), channel_id=1, source_target_pairs={{1,0},{2,1},{3,2},{16,3},{17,16},{18,17},{19,18},{32,19},{33,32},{... | collective-permute-start | bytes 52232 | tf_op jit(solution)/shard_map/ppermute | solution.py:24
  116.4 2.5 %reshape.236 = bf16[256,24,40]{2,1,0:T(8,128)(2,1)S(1)} reshape(bf16[64,2,1920]{2,1,0:T(2,128)(2,1)S(1)} %all-to-all-done) | data formatting | bytes 983040
  119.0 0.6 copy.33
  119.6 3.9 %all_to_all.16 = bf16[4,24,2560]{2,1,0:T(8,128)(2,1)} reshape(bf16[4,24,64,40]{3,2,1,0:T(8,128)(2,1)S(1)} %copy.33) | data formatting | bytes 983040 | tf_op jit(solution)/shard_map/all_to_all | solution.py:65
  123.4 0.0 all-gather.2.cloned.1.call-update
  123.5 0.1 fusion.23
  123.6 0.1 fusion.35
  123.7 0.1 broadcast_in_dim.66
  123.9 0.0 collective-permute-done
  123.9 25.7 %all-reduce.5.cloned.1.call-done = f32[2,16,2176]{2,1,0:T(8,128)} async-done(((f32[2,16,2176]{2,1,0:T(8,128)}), f32[2,16,2176]{2,1,0:T(8,128)}) %all-reduce.5.cloned.1.call-update) | async-done | bytes 278544 | tf_op jit(solution)/shard_map/psum | solution.py:99
  149.5 1.2 fusion.31
  150.7 0.7 slice_bitcast_fusion
  151.4 8.4 %collective-permute-start.5 = (f32[16,2176]{1,0:T(8,128)S(1)}, f32[16,2176]{1,0:T(8,128)S(1)}, u32[]{:S(2)}, u32[]{:S(2)}) collective-permute-start(f32[16,2176]{1,0:T(8,128)S(1)} %get-tuple-element.11), channel_id=1, source_target_pairs={{1,0},{2,1},{3,2},{16,3},{17,16},{18,17},{19,18},{32,19},{33,32},{... | collective-permute-start | bytes 417800 | tf_op jit(solution)/shard_map/ppermute | solution.py:24
  159.8 1.9 collective-permute-start.4
  161.7 0.1 copy.39
  161.9 2.9 %collective-permute-done.5 = f32[16,2176]{1,0:T(8,128)S(1)} collective-permute-done((f32[16,2176]{1,0:T(8,128)S(1)}, f32[16,2176]{1,0:T(8,128)S(1)}, u32[]{:S(2)}, u32[]{:S(2)}) %collective-permute-start.5) | collective-permute-done | bytes 139296 | tf_op jit(solution)/shard_map/ppermute | solution.py:24
  164.8 5.0 %collective-permute-done.4 = f32[16,2176]{1,0:T(8,128)S(1)} collective-permute-done((f32[16,2176]{1,0:T(8,128)S(1)}, f32[16,2176]{1,0:T(8,128)S(1)}, u32[]{:S(2)}, u32[]{:S(2)}) %collective-permute-start.4) | collective-permute-done | bytes 139296 | tf_op jit(solution)/shard_map/ppermute | solution.py:22
  169.8 1.2 gather_fusion
  171.1 0.1 broadcast_in_dim.68
  171.2 0.8 select_select_fusion
  172.0 14.7 %all-gather.2.cloned.1.call-done = bf16[4,96,2560]{2,1,0:T(8,128)(2,1)} async-done(((bf16[4,24,2560]{2,1,0:T(8,128)(2,1)}), bf16[4,96,2560]{2,1,0:T(8,128)(2,1)}) %all-gather.2.cloned.1.call-update) | async-done | bytes 1966096 | tf_op jit(solution)/shard_map/all_gather | solution.py:74
  186.7 6.1 %fusion.44 = f32[4,96,384]{2,1,0:T(8,128)} fusion(bf16[4,96,2560]{2,1,0:T(8,128)(2,1)} %all-gather.2.cloned.1.call-done, bf16[4,2560,384]{2,1,0:T(8,128)(2,1)} %param.12), kind=kOutput, calls=%fused_computation.87 | convolution fusion | flops 754974720 | bytes 10420224 | tf_op jit(solution)/shard_map/srj,sjd->srd/dot_general | solution.py:72
  (34 shorter events, 0.4 us)
Async XLA Ops:
  7.2 4.5 %copy-start = (bf16[2,6]{1,0:T(2,128)(2,1)S(1)}, bf16[2,6]{1,0:T(2,128)(2,1)}, u32[]{:S(2)}) copy-start(bf16[2,6]{1,0:T(2,128)(2,1)} %param.13) | copy-start | bytes 76
  7.2 71.3 %all-reduce.3.cloned.1.call-start = ((), (), s32[]{:S(2)}) async-start(), calls=%async_computation.2 | async-start | bytes 3604480 | tf_op jit(solution)/shard_map/psum | solution.py:87
  11.7 3.8 %copy-start.1 = (bf16[2,6,40,5632]{3,2,1,0:T(8,128)(2,1)}, bf16[2,6,40,5632]{3,2,1,0:T(8,128)(2,1)S(1)}, u32[]{:S(2)}) copy-start(bf16[2,6,40,5632]{3,2,1,0:T(8,128)(2,1)S(1)} %broadcast_select_fusion) | copy-start | bytes 16220164
  11.7 3.8 %copy-start.7 = (s32[40]{0:T(128)S(1)}, s32[40]{0:T(128)}, u32[]{:S(2)}) copy-start(s32[40]{0:T(128)} %param.10) | copy-start | bytes 484
  11.7 3.8 %copy-start.8 = (s32[256]{0:T(256)S(1)}, s32[256]{0:T(256)}, u32[]{:S(2)}) copy-start(s32[256]{0:T(256)} %param.11) | copy-start | bytes 3076
  15.6 28.0 %slice-start = ((s8[5406720]{0:T(1024)(128)(4,1)}), s8[4194304]{0:T(1024)(128)(4,1)S(1)}, s32[]{:S(2)}) async-start(s8[5406720]{0:T(1024)(128)(4,1)} %bitcast.60), calls=%async_computation.4 | async-start | bytes 8388608
  40.6 3.0 %slice-start.1 = ((s8[5406720]{0:T(1024)(128)(4,1)}), s8[1212416]{0:T(1024)(128)(4,1)S(1)}, s32[]{:S(2)}) async-start(s8[5406720]{0:T(1024)(128)(4,1)} %bitcast.60), calls=%async_computation.5 | async-start | bytes 2424832
  49.3 17.8 %copy-start.5 = (s32[40,11]{0,1:T(8,128)S(1)}, s32[40,11]{0,1:T(8,128)}, u32[]{:S(2)}) copy-start(s32[40,11]{0,1:T(8,128)} %param.14) | copy-start | bytes 5284
  53.7 54.9 %copy-start.2 = (f32[16,2176]{1,0:T(8,128)S(1)}, f32[16,2176]{1,0:T(8,128)}, u32[]{:S(2)}) copy-start(f32[16,2176]{1,0:T(8,128)} %param.15) | copy-start | bytes 417796
  53.7 54.9 %copy-start.3 = (f32[16,2176]{1,0:T(8,128)S(1)}, f32[16,2176]{1,0:T(8,128)}, u32[]{:S(2)}) copy-start(f32[16,2176]{1,0:T(8,128)} %param.16) | copy-start | bytes 417796
  53.7 62.7 %all-to-all-start = ((bf16[64,2,1920]{2,1,0:T(2,128)(2,1)}), bf16[64,2,1920]{2,1,0:T(2,128)(2,1)S(1)}, u32[]{:S(2)}, u32[]{:S(2)}) async-start(bf16[64,2,1920]{2,1,0:T(2,128)(2,1)} %reshape.235), calls=%async_computation | async-start | bytes 983040 | tf_op jit(solution)/shard_map/all_to_all | solution.py:65
  67.1 82.5 %all-reduce.5.cloned.1.call-start = ((), (), s32[]{:S(2)}) async-start(), calls=%async_computation.3 | async-start | bytes 557056 | tf_op jit(solution)/shard_map/psum | solution.py:99
  83.2 16.4 %collective-permute-start.3 = (f32[272,256]{1,0:T(8,128)S(1)}, f32[272,256]{1,0:T(8,128)S(1)}, u32[]{:S(2)}, u32[]{:S(2)}) collective-permute-start(f32[272,256]{1,0:T(8,128)S(1)} %get-tuple-element.9), channel_id=1, source_target_pairs={{1,0},{2,1},{3,2},{16,3},{17,16},{18,17},{19,18},{32,19},{33,32},{... | collective-permute-start | bytes 835592 | tf_op jit(solution)/shard_map/ppermute | solution.py:24
  89.5 18.1 %collective-permute-start.2 = (f32[272,256]{1,0:T(8,128)S(1)}, f32[272,256]{1,0:T(8,128)S(1)}, u32[]{:S(2)}, u32[]{:S(2)}) collective-permute-start(f32[272,256]{1,0:T(8,128)S(1)} %get-tuple-element.8), channel_id=1, source_target_pairs={{0,1},{1,2},{2,3},{3,16},{16,17},{17,18},{18,19},{19,32},{32,33},{... | collective-permute-start | bytes 835592 | tf_op jit(solution)/shard_map/ppermute | solution.py:22
  107.6 15.8 %copy-start.6 = (s32[16,17]{1,0:T(8,128)S(1)}, s32[16,17]{1,0:T(8,128)}, u32[]{:S(2)}) copy-start(s32[16,17]{1,0:T(8,128)} %param.17) | copy-start | bytes 3268
  108.6 78.1 %all-gather.2.cloned.1.call-start = ((), (), s32[]{:S(2)}) async-start(), calls=%async_computation.1 | async-start | bytes 2457600 | tf_op jit(solution)/shard_map/all_gather | solution.py:74
  108.7 15.1 %collective-permute-start.1 = (f32[2,1,2176]{2,1,0:T(1,128)S(1)}, f32[2,1,2176]{2,1,0:T(1,128)S(1)}, u32[]{:S(2)}, u32[]{:S(2)}) collective-permute-start(f32[2,1,2176]{2,1,0:T(1,128)S(1)} %get-tuple-element.17), channel_id=1, source_target_pairs={{0,1},{1,2},{2,3},{3,16},{16,17},{17,18},{18,19},{19,32},{32,33},{... | collective-permute-start | bytes 52232 | tf_op jit(solution)/shard_map/ppermute | solution.py:22
  110.7 13.2 %collective-permute-start = (f32[2,1,2176]{2,1,0:T(1,128)S(1)}, f32[2,1,2176]{2,1,0:T(1,128)S(1)}, u32[]{:S(2)}, u32[]{:S(2)}) collective-permute-start(f32[2,1,2176]{2,1,0:T(1,128)S(1)} %get-tuple-element.16), channel_id=1, source_target_pairs={{1,0},{2,1},{3,2},{16,3},{17,16},{18,17},{19,18},{32,19},{33,32},{... | collective-permute-start | bytes 52232 | tf_op jit(solution)/shard_map/ppermute | solution.py:24
  151.4 41.4 %copy-start.4 = (f32[16,2176]{1,0:T(8,128)}, f32[16,2176]{1,0:T(8,128)S(1)}, u32[]{:S(2)}) copy-start(f32[16,2176]{1,0:T(8,128)S(1)} %get-tuple-element.11) | copy-start | bytes 417796
  151.4 13.4 %collective-permute-start.5 = (f32[16,2176]{1,0:T(8,128)S(1)}, f32[16,2176]{1,0:T(8,128)S(1)}, u32[]{:S(2)}, u32[]{:S(2)}) collective-permute-start(f32[16,2176]{1,0:T(8,128)S(1)} %get-tuple-element.11), channel_id=1, source_target_pairs={{1,0},{2,1},{3,2},{16,3},{17,16},{18,17},{19,18},{32,19},{33,32},{... | collective-permute-start | bytes 417800 | tf_op jit(solution)/shard_map/ppermute | solution.py:24
  159.8 10.0 %collective-permute-start.4 = (f32[16,2176]{1,0:T(8,128)S(1)}, f32[16,2176]{1,0:T(8,128)S(1)}, u32[]{:S(2)}, u32[]{:S(2)}) collective-permute-start(f32[16,2176]{1,0:T(8,128)S(1)} %get-tuple-element.11), channel_id=1, source_target_pairs={{0,1},{1,2},{2,3},{3,16},{16,17},{17,18},{18,19},{19,32},{32,33},{... | collective-permute-start | bytes 417800 | tf_op jit(solution)/shard_map/ppermute | solution.py:22
Sparse Core Ops, SparseCore 0:
  15.7 62.7 all-reduce.2
  108.7 40.7 all-reduce.4
  152.1 34.6 all-gather.1
where the time goes:
time: 200 us; the launch traced here: 199 us
  waiting for transfers between devices  75.1 us (38%)
  starting transfers between devices  39.7 us (20%)
  other arithmetic  37.9 us (19%)
  local copies, waits for them, and re-layouts  18.2 us (9%)
  matrix products  14.2 us (7%)
  between operations  14.2 us (7%)
    psum x1, waiting for transfers between devices, body(): tile_sums = lax.psum(arrived, 'lev')  25.7 us
    another operation x1, other arithmetic  25 us
    ppermute x3, starting transfers between devices, with_halo(): lax.ppermute(head, axis, [((i + 1) % count, i) for i in range(ends)])  20.5 us
    all_gather x1, waiting for transfers between devices, body(): lax.all_gather(regrouped, 'lev', axis=1, tiled=True)  14.7 us
    all_to_all x1, starting transfers between devices, body(): lax.all_to_all(coeffs.transpose(4, 1, 0, 3, 2).reshape(wave_count, lev_de...  13.3 us
    ppermute x3, waiting for transfers between devices, with_halo(): lax.ppermute(tail, axis, [(i, (i + 1) % count) for i in range(ends)])  13 us
    ppermute x3, waiting for transfers between devices, with_halo(): lax.ppermute(head, axis, [((i + 1) % count, i) for i in range(ends)])  11.1 us
    psum x1, waiting for transfers between devices, body(): totals = lax.psum(partial_sum, 'lev')  10.6 us
  transfers between devices with their start and end apart: 10, of which 7 were waited for; matrix products, arithmetic and copies ran while one was open for 26% of the time, Pallas kernels for 0%

commit v1 on v0

--- a/solution.py
+++ b/solution.py
@@ -71,7 +71,9 @@
     )
     spectra = jnp.einsum(
         "srj,sjd->srd",
-        lax.all_gather(regrouped, "lev", axis=1, tiled=True),
+        jnp.concatenate(
+            lax.all_to_all(jnp.stack([regrouped] * lax.axis_size("lev")), "lev", 0, 0), axis=1
+        ),
         legendre,
         preferred_element_type=jnp.float32,
     )

time: 200 us -> 183 us (0.915); the launches traced: 199 us -> 180 us
  waiting for transfers between devices: 75.1 us -> 50.7 us
  starting transfers between devices: 39.7 us -> 43.1 us
    all_gather x1 -> x0, waiting for transfers between devices: 14.7 us -> none  [body(): lax.all_gather(regrouped, 'lev', axis=1, tiled=True)]
    psum x1, waiting for transfers between devices: 10.6 us -> 2.4 us  [body(): totals = lax.psum(partial_sum, 'lev')]
    psum x1, waiting for transfers between devices: 25.7 us -> 30.3 us  [body(): tile_sums = lax.psum(arrived, 'lev')]
    another operation x0 -> x2, local copies, waits for them, and re-layouts: none -> 4.52 us  [body(): jnp.stack([regrouped] * lax.axis_size('lev'))]
    all_to_all x2 -> x1, local copies, waits for them, and re-layouts: 4.47 us -> 0.61 us  [body(): lax.all_to_all(coeffs.transpose(4, 1, 0, 3, 2).reshape(wave_count, lev_de...]
    ppermute x3, waiting for transfers between devices: 11.1 us -> 7.27 us  [with_halo(): lax.ppermute(head, axis, [((i + 1) % count, i) for i in range(ends)])]
    all_to_all x0 -> x1, starting transfers between devices: none -> 3.6 us  [body(): lax.all_to_all(jnp.stack([regrouped] * lax.axis_size('lev')), 'lev', 0, 0)]
    ppermute x3, waiting for transfers between devices: 13 us -> 10.6 us  [with_halo(): lax.ppermute(tail, axis, [(i, (i + 1) % count) for i in range(ends)])]
  transfers between devices with their start and end apart: 10 -> 10, of which waited for: 7 -> 5; matrix products, arithmetic and copies ran while one was open for 26% -> 34% of each run, Pallas kernels for 0% -> 0%
where the time goes in v1:
time: 183 us; the launch traced here: 180 us
  waiting for transfers between devices  50.7 us (28%)
  starting transfers between devices  43.1 us (24%)
  other arithmetic  39.4 us (22%)
  local copies, waits for them, and re-layouts  19 us (10%)
  between operations  14.5 us (8%)
  matrix products  13.6 us (7%)
    psum x1, waiting for transfers between devices, body(): tile_sums = lax.psum(arrived, 'lev')  30.3 us
    another operation x1, other arithmetic  25 us
    ppermute x3, starting transfers between devices, with_halo(): lax.ppermute(head, axis, [((i + 1) % count, i) for i in range(ends)])  18.2 us
    all_to_all x1, starting transfers between devices, body(): lax.all_to_all(coeffs.transpose(4, 1, 0, 3, 2).reshape(wave_count, lev_de...  13.2 us
    ppermute x3, waiting for transfers between devices, with_halo(): lax.ppermute(tail, axis, [(i, (i + 1) % count) for i in range(ends)])  10.6 us
    ppermute x3, starting transfers between devices, with_halo(): lax.ppermute(tail, axis, [(i, (i + 1) % count) for i in range(ends)])  8.02 us
    ppermute x3, waiting for transfers between devices, with_halo(): lax.ppermute(head, axis, [((i + 1) % count, i) for i in range(ends)])  7.27 us
    unnamed x25, local copies, waits for them, and re-layouts  6.01 us
  transfers between devices with their start and end apart: 10, of which 5 were waited for; matrix products, arithmetic and copies ran while one was open for 34% of the time, Pallas kernels for 0%

profile of v1, /device:TPU:1, one launch (start us, length us, event | category | flops | bytes accessed | tf_op | source)
XLA Modules:
  0.0 180.3 jit_solution(8099330431604696891)
XLA Ops:
  7.2 0.0 copy-start
  7.2 0.0 all-reduce.3.cloned.1.call-start
  7.2 0.8 iota_compare_fusion
  8.1 3.6 %broadcast_select_fusion = bf16[2,6,40,5632]{3,2,1,0:T(8,128)(2,1)S(1)} fusion(bf16[2,6,40,5632]{3,2,1,0:T(8,128)(2,1)} %param.9, pred[40,5632]{1,0:T(8,128)(4,1)S(1)} %iota_compare_fusion), kind=kLoop, calls=%fused_computation.16 | loop fusion | flops 2703360 | bytes 11038720 | tf_op jit(solution)/shard_map/jit(_where)/select_n | solution.py:54
  11.7 0.0 copy-start.7
  11.7 0.0 copy-start.8
  11.7 2.4 %fusion = f32[2,1,40,5632]{3,1,2,0:T(1,128)S(1)} fusion(bf16[2,6,40,5632]{3,2,1,0:T(8,128)(2,1)S(1)} %broadcast_select_fusion, bf16[2,6,1,1]{1,0,2,3:T(2,128)(2,1)S(1)} %bitcast.61), kind=kOutput, calls=%fused_computation.3 | convolution fusion | flops 5406720 | bytes 7208984 | tf_op jit(solution)/shard_map/ql,qljk->qjk/dot_general | solution.py:85
  14.2 1.3 copy.60
  15.5 0.0 all-reduce.3.cloned.1.call-update
  15.6 0.0 slice-start
  15.6 25.0 %cosine_convert_fusion = (bf16[5632,256]{0,1:T(8,128)(2,1)S(1)}, bf16[5632,256]{0,1:T(8,128)(2,1)S(1)}) fusion(s32[256]{0:T(256)S(1)} %copy-done.8), kind=kLoop, calls=%fused_computation.9 | loop fusion | flops 17301504 | bytes 5768192 | tf_op jit(solution)/shard_map/convert
  40.6 2.9 %pad_maximum_fusion = bf16[5632,512]{0,1:T(8,128)(2,1)} fusion(bf16[5632,256]{0,1:T(8,128)(2,1)S(1)} %get-tuple-element.21, bf16[5632,256]{0,1:T(8,128)(2,1)S(1)} %get-tuple-element.20), kind=kLoop, calls=%fused_computation.7 | loop fusion | flops 11534336 | bytes 11534336 | tf_op jit(solution)/shard_map/concatenate | solution.py:35
  43.5 0.1 compare_select_fusion
  43.6 5.7 %fusion.15 = bf16[256,6,2,2,40]{0,4,3,1,2:T(8,128)(2,1)S(1)} fusion(bf16[2,256,5632,1,1]{2,1,0,4,3:T(8,128)(2,1)} %bitcast.68, bf16[2,6,40,5632]{3,2,1,0:T(8,128)(2,1)S(1)} %bitcast.63, f32[256,40]{0,1:T(8,128)S(1)} %compare_select_fusion), kind=kOutput, calls=%fused_computation.20 | convolution fusion | flops 2768732160 | bytes 11706368 | tf_op jit(solution)/shard_map/dot_general | solution.py:62
  49.3 0.0 copy-start.2
  49.3 0.0 copy-start.3
  49.3 0.0 copy-start.5
  49.4 1.0 copy.32
  50.4 0.0 copy-start.6
  50.4 3.4 %reshape.246 = bf16[64,2,1920]{2,1,0:T(2,128)(2,1)} reshape(bf16[256,24,40]{2,1,0:T(8,128)(2,1)S(1)} %copy.32) | data formatting | bytes 983040
  53.8 13.2 %all-to-all-start = ((bf16[64,2,1920]{2,1,0:T(2,128)(2,1)}), bf16[64,2,1920]{2,1,0:T(2,128)(2,1)S(1)}, u32[]{:S(2)}, u32[]{:S(2)}) async-start(bf16[64,2,1920]{2,1,0:T(2,128)(2,1)} %reshape.246), calls=%async_computation | async-start | bytes 983040 | tf_op jit(solution)/shard_map/all_to_all | solution.py:65
  67.0 0.0 all-reduce.5.cloned.1.call-start
  67.0 0.6 fusion.32
  67.7 4.2 %collective-permute-start.1 = (f32[2,1,2176]{2,1,0:T(1,128)}, f32[2,1,2176]{2,1,0:T(1,128)S(1)}, u32[]{:S(2)}, u32[]{:S(2)}) collective-permute-start(f32[2,1,2176]{2,1,0:T(1,128)} %get-tuple-element.17), channel_id=1, source_target_pairs={{0,1},{1,2},{2,3},{3,16},{16,17},{17,18},{18,19},{19,32},{32,33},{... | collective-permute-start | bytes 52232 | tf_op jit(solution)/shard_map/ppermute | solution.py:22
  71.9 3.5 %collective-permute-start = (f32[2,1,2176]{2,1,0:T(1,128)S(1)}, f32[2,1,2176]{2,1,0:T(1,128)S(1)}, u32[]{:S(2)}, u32[]{:S(2)}) collective-permute-start(f32[2,1,2176]{2,1,0:T(1,128)S(1)} %get-tuple-element.16), channel_id=1, source_target_pairs={{1,0},{2,1},{3,2},{16,3},{17,16},{18,17},{19,18},{32,19},{33,32},{... | collective-permute-start | bytes 52232 | tf_op jit(solution)/shard_map/ppermute | solution.py:24
  75.4 0.1 copy.36
  75.5 0.1 rem.47
  75.6 0.1 copy.37
  75.7 0.1 div.26
  75.8 0.1 copy.35
  75.9 0.1 ne.88
  76.1 2.4 %all-reduce.3.cloned.1.call-done = f32[2,40,5632]{2,1,0:T(8,128)} async-done(((f32[2,40,5632]{2,1,0:T(8,128)}), f32[2,40,5632]{2,1,0:T(8,128)}) %all-reduce.3.cloned.1.call-update) | async-done | bytes 1802256 | tf_op jit(solution)/shard_map/psum | solution.py:89
  78.5 1.0 constant_dynamic-slice_fusion
  79.5 0.1 reshape.219
  79.6 0.3 copy.38
  80.0 3.1 %scatter_custom_fusion = f32[816,256]{1,0:T(8,128)S(1)} fusion(s32[440]{0:T(512)S(1)} %bitcast.85, f32[55,8,2,128]{3,2,1,0:T(2,128)S(1)} %bitcast.79, f32[]{:T(128)} %constant.40.clone.1), kind=kCustom, calls=%fused_computation.35 | custom fusion | flops 112640 | bytes 1286148 | tf_op jit(solution)/shard_map/scatter-add | solution.py:96
  83.2 6.3 %collective-permute-start.3 = (f32[272,256]{1,0:T(8,128)S(1)}, f32[272,256]{1,0:T(8,128)S(1)}, u32[]{:S(2)}, u32[]{:S(2)}) collective-permute-start(f32[272,256]{1,0:T(8,128)S(1)} %get-tuple-element.9), channel_id=1, source_target_pairs={{1,0},{2,1},{3,2},{16,3},{17,16},{18,17},{19,18},{32,19},{33,32},{... | collective-permute-start | bytes 835592 | tf_op jit(solution)/shard_map/ppermute | solution.py:24
  89.5 1.9 %collective-permute-start.2 = (f32[272,256]{1,0:T(8,128)S(1)}, f32[272,256]{1,0:T(8,128)S(1)}, u32[]{:S(2)}, u32[]{:S(2)}) collective-permute-start(f32[272,256]{1,0:T(8,128)S(1)} %get-tuple-element.8), channel_id=1, source_target_pairs={{0,1},{1,2},{2,3},{3,16},{16,17},{17,18},{18,19},{19,32},{32,33},{... | collective-permute-start | bytes 835592 | tf_op jit(solution)/shard_map/ppermute | solution.py:22
  91.4 0.9 fusion.23
  92.3 7.3 %collective-permute-done.3 = f32[272,256]{1,0:T(8,128)S(1)} collective-permute-done((f32[272,256]{1,0:T(8,128)S(1)}, f32[272,256]{1,0:T(8,128)S(1)}, u32[]{:S(2)}, u32[]{:S(2)}) %collective-permute-start.3) | collective-permute-done | bytes 278560 | tf_op jit(solution)/shard_map/ppermute | solution.py:24
  99.6 8.0 %collective-permute-done.2 = f32[272,256]{1,0:T(8,128)S(1)} collective-permute-done((f32[272,256]{1,0:T(8,128)S(1)}, f32[272,256]{1,0:T(8,128)S(1)}, u32[]{:S(2)}, u32[]{:S(2)}) %collective-permute-start.2) | collective-permute-done | bytes 278560 | tf_op jit(solution)/shard_map/ppermute | solution.py:22
  107.6 0.1 fusion.24
  107.6 0.1 reshape.221
  107.8 0.8 reshape.222
  108.6 0.0 all-reduce.5.cloned.1.call-update
  108.6 0.1 fusion.35
  108.7 2.5 %reshape.247 = bf16[256,24,40]{2,1,0:T(8,128)(2,1)S(1)} reshape(bf16[64,2,1920]{2,1,0:T(2,128)(2,1)S(1)} %all-to-all-done) | data formatting | bytes 983040
  111.2 0.6 copy.33
  111.8 3.1 %stack.18 = bf16[4,24,2560]{2,1,0:T(8,128)(2,1)S(1)} reshape(bf16[4,24,64,40]{3,2,1,0:T(8,128)(2,1)S(1)} %copy.33) | data formatting | bytes 983040 | tf_op jit(solution)/shard_map/stack | solution.py:75
  114.9 1.4 stack.19
  116.4 3.6 %all-to-all-start.1 = ((bf16[4,4,24,2560]{3,2,1,0:T(8,128)(2,1)}), bf16[4,4,24,2560]{3,2,1,0:T(8,128)(2,1)S(1)}, u32[]{:S(2)}, u32[]{:S(2)}) async-start(bf16[4,4,24,2560]{3,2,1,0:T(8,128)(2,1)} %stack.19), calls=%async_computation.1 | async-start | bytes 3932160 | tf_op jit(solution)/shard_map/all_to_all | solution.py:75
  120.0 0.1 broadcast_in_dim.66
  120.1 0.1 copy.40
  120.3 30.3 %all-reduce.5.cloned.1.call-done = f32[2,16,2176]{2,1,0:T(8,128)} async-done(((f32[2,16,2176]{2,1,0:T(8,128)}), f32[2,16,2176]{2,1,0:T(8,128)}) %all-reduce.5.cloned.1.call-update) | async-done | bytes 278544 | tf_op jit(solution)/shard_map/psum | solution.py:101
  150.6 1.3 fusion.31
  151.9 0.7 slice_bitcast_fusion
  152.6 8.4 %collective-permute-start.5 = (f32[16,2176]{1,0:T(8,128)S(1)}, f32[16,2176]{1,0:T(8,128)S(1)}, u32[]{:S(2)}, u32[]{:S(2)}) collective-permute-start(f32[16,2176]{1,0:T(8,128)S(1)} %get-tuple-element.11), channel_id=1, source_target_pairs={{1,0},{2,1},{3,2},{16,3},{17,16},{18,17},{19,18},{32,19},{33,32},{... | collective-permute-start | bytes 417800 | tf_op jit(solution)/shard_map/ppermute | solution.py:24
  161.0 1.9 %collective-permute-start.4 = (f32[16,2176]{1,0:T(8,128)S(1)}, f32[16,2176]{1,0:T(8,128)S(1)}, u32[]{:S(2)}, u32[]{:S(2)}) collective-permute-start(f32[16,2176]{1,0:T(8,128)S(1)} %get-tuple-element.11), channel_id=1, source_target_pairs={{0,1},{1,2},{2,3},{3,16},{16,17},{17,18},{18,19},{19,32},{32,33},{... | collective-permute-start | bytes 417800 | tf_op jit(solution)/shard_map/ppermute | solution.py:22
  163.0 0.2 copy.34
  163.1 5.5 %fusion.44 = f32[4,96,384]{2,1,0:T(8,128)} fusion(bf16[4,96,2560]{2,1,0:T(8,128)(2,1)S(1)} %bitcast.64, bf16[4,2560,384]{2,1,0:T(8,128)(2,1)} %param.12), kind=kOutput, calls=%fused_computation.87 | convolution fusion | flops 754974720 | bytes 10420224 | tf_op jit(solution)/shard_map/srj,sjd->srd/dot_general | solution.py:72
  168.6 2.7 %collective-permute-done.4 = f32[16,2176]{1,0:T(8,128)S(1)} collective-permute-done((f32[16,2176]{1,0:T(8,128)S(1)}, f32[16,2176]{1,0:T(8,128)S(1)}, u32[]{:S(2)}, u32[]{:S(2)}) %collective-permute-start.4) | collective-permute-done | bytes 139296 | tf_op jit(solution)/shard_map/ppermute | solution.py:22
  171.3 1.2 gather_fusion
  172.5 0.1 broadcast_in_dim.68
  172.7 0.8 select_select_fusion
  (35 shorter events, 0.4 us)
Async XLA Ops:
  7.2 4.5 %copy-start = (bf16[2,6]{1,0:T(2,128)(2,1)S(1)}, bf16[2,6]{1,0:T(2,128)(2,1)}, u32[]{:S(2)}) copy-start(bf16[2,6]{1,0:T(2,128)(2,1)} %param.13) | copy-start | bytes 76
  7.2 71.3 %all-reduce.3.cloned.1.call-start = ((), (), s32[]{:S(2)}) async-start(), calls=%async_computation.2 | async-start | bytes 3604480 | tf_op jit(solution)/shard_map/psum | solution.py:89
  11.7 3.8 %copy-start.1 = (bf16[2,6,40,5632]{3,2,1,0:T(8,128)(2,1)}, bf16[2,6,40,5632]{3,2,1,0:T(8,128)(2,1)S(1)}, u32[]{:S(2)}) copy-start(bf16[2,6,40,5632]{3,2,1,0:T(8,128)(2,1)S(1)} %broadcast_select_fusion) | copy-start | bytes 16220164
  11.7 3.8 %copy-start.7 = (s32[40]{0:T(128)S(1)}, s32[40]{0:T(128)}, u32[]{:S(2)}) copy-start(s32[40]{0:T(128)} %param.10) | copy-start | bytes 484
  11.7 3.8 %copy-start.8 = (s32[256]{0:T(256)S(1)}, s32[256]{0:T(256)}, u32[]{:S(2)}) copy-start(s32[256]{0:T(256)} %param.11) | copy-start | bytes 3076
  15.6 28.0 %slice-start = ((s8[5406720]{0:T(1024)(128)(4,1)}), s8[4194304]{0:T(1024)(128)(4,1)S(1)}, s32[]{:S(2)}) async-start(s8[5406720]{0:T(1024)(128)(4,1)} %bitcast.62), calls=%async_computation.4 | async-start | bytes 8388608
  40.6 3.0 %slice-start.1 = ((s8[5406720]{0:T(1024)(128)(4,1)}), s8[1212416]{0:T(1024)(128)(4,1)S(1)}, s32[]{:S(2)}) async-start(s8[5406720]{0:T(1024)(128)(4,1)} %bitcast.62), calls=%async_computation.5 | async-start | bytes 2424832
  49.3 17.7 %copy-start.2 = (f32[16,2176]{1,0:T(8,128)S(1)}, f32[16,2176]{1,0:T(8,128)}, u32[]{:S(2)}) copy-start(f32[16,2176]{1,0:T(8,128)} %param.15) | copy-start | bytes 417796
  49.3 17.7 %copy-start.3 = (f32[16,2176]{1,0:T(8,128)S(1)}, f32[16,2176]{1,0:T(8,128)}, u32[]{:S(2)}) copy-start(f32[16,2176]{1,0:T(8,128)} %param.16) | copy-start | bytes 417796
  49.3 26.0 %copy-start.5 = (s32[40,11]{0,1:T(8,128)S(1)}, s32[40,11]{0,1:T(8,128)}, u32[]{:S(2)}) copy-start(s32[40,11]{0,1:T(8,128)} %param.14) | copy-start | bytes 5284
  50.4 41.9 %copy-start.6 = (s32[16,17]{1,0:T(8,128)S(1)}, s32[16,17]{1,0:T(8,128)}, u32[]{:S(2)}) copy-start(s32[16,17]{1,0:T(8,128)} %param.17) | copy-start | bytes 3268
  53.8 54.9 %all-to-all-start = ((bf16[64,2,1920]{2,1,0:T(2,128)(2,1)}), bf16[64,2,1920]{2,1,0:T(2,128)(2,1)S(1)}, u32[]{:S(2)}, u32[]{:S(2)}) async-start(bf16[64,2,1920]{2,1,0:T(2,128)(2,1)} %reshape.246), calls=%async_computation | async-start | bytes 983040 | tf_op jit(solution)/shard_map/all_to_all | solution.py:65
  67.0 83.6 %all-reduce.5.cloned.1.call-start = ((), (), s32[]{:S(2)}) async-start(), calls=%async_computation.3 | async-start | bytes 557056 | tf_op jit(solution)/shard_map/psum | solution.py:101
  67.7 52.6 %collective-permute-start.1 = (f32[2,1,2176]{2,1,0:T(1,128)}, f32[2,1,2176]{2,1,0:T(1,128)S(1)}, u32[]{:S(2)}, u32[]{:S(2)}) collective-permute-start(f32[2,1,2176]{2,1,0:T(1,128)} %get-tuple-element.17), channel_id=1, source_target_pairs={{0,1},{1,2},{2,3},{3,16},{16,17},{17,18},{18,19},{19,32},{32,33},{... | collective-permute-start | bytes 52232 | tf_op jit(solution)/shard_map/ppermute | solution.py:22
  71.9 48.4 %collective-permute-start = (f32[2,1,2176]{2,1,0:T(1,128)S(1)}, f32[2,1,2176]{2,1,0:T(1,128)S(1)}, u32[]{:S(2)}, u32[]{:S(2)}) collective-permute-start(f32[2,1,2176]{2,1,0:T(1,128)S(1)} %get-tuple-element.16), channel_id=1, source_target_pairs={{1,0},{2,1},{3,2},{16,3},{17,16},{18,17},{19,18},{32,19},{33,32},{... | collective-permute-start | bytes 52232 | tf_op jit(solution)/shard_map/ppermute | solution.py:24
  83.2 16.4 %collective-permute-start.3 = (f32[272,256]{1,0:T(8,128)S(1)}, f32[272,256]{1,0:T(8,128)S(1)}, u32[]{:S(2)}, u32[]{:S(2)}) collective-permute-start(f32[272,256]{1,0:T(8,128)S(1)} %get-tuple-element.9), channel_id=1, source_target_pairs={{1,0},{2,1},{3,2},{16,3},{17,16},{18,17},{19,18},{32,19},{33,32},{... | collective-permute-start | bytes 835592 | tf_op jit(solution)/shard_map/ppermute | solution.py:24
  89.5 18.1 %collective-permute-start.2 = (f32[272,256]{1,0:T(8,128)S(1)}, f32[272,256]{1,0:T(8,128)S(1)}, u32[]{:S(2)}, u32[]{:S(2)}) collective-permute-start(f32[272,256]{1,0:T(8,128)S(1)} %get-tuple-element.8), channel_id=1, source_target_pairs={{0,1},{1,2},{2,3},{3,16},{16,17},{17,18},{18,19},{19,32},{32,33},{... | collective-permute-start | bytes 835592 | tf_op jit(solution)/shard_map/ppermute | solution.py:22
  116.4 46.6 %all-to-all-start.1 = ((bf16[4,4,24,2560]{3,2,1,0:T(8,128)(2,1)}), bf16[4,4,24,2560]{3,2,1,0:T(8,128)(2,1)S(1)}, u32[]{:S(2)}, u32[]{:S(2)}) async-start(bf16[4,4,24,2560]{3,2,1,0:T(8,128)(2,1)} %stack.19), calls=%async_computation.1 | async-start | bytes 3932160 | tf_op jit(solution)/shard_map/all_to_all | solution.py:75
  152.6 18.7 %copy-start.4 = (f32[16,2176]{1,0:T(8,128)}, f32[16,2176]{1,0:T(8,128)S(1)}, u32[]{:S(2)}) copy-start(f32[16,2176]{1,0:T(8,128)S(1)} %get-tuple-element.11) | copy-start | bytes 417796
  152.6 16.0 %collective-permute-start.5 = (f32[16,2176]{1,0:T(8,128)S(1)}, f32[16,2176]{1,0:T(8,128)S(1)}, u32[]{:S(2)}, u32[]{:S(2)}) collective-permute-start(f32[16,2176]{1,0:T(8,128)S(1)} %get-tuple-element.11), channel_id=1, source_target_pairs={{1,0},{2,1},{3,2},{16,3},{17,16},{18,17},{19,18},{32,19},{33,32},{... | collective-permute-start | bytes 417800 | tf_op jit(solution)/shard_map/ppermute | solution.py:24
  161.0 10.2 %collective-permute-start.4 = (f32[16,2176]{1,0:T(8,128)S(1)}, f32[16,2176]{1,0:T(8,128)S(1)}, u32[]{:S(2)}, u32[]{:S(2)}) collective-permute-start(f32[16,2176]{1,0:T(8,128)S(1)} %get-tuple-element.11), channel_id=1, source_target_pairs={{0,1},{1,2},{2,3},{3,16},{16,17},{17,18},{18,19},{19,32},{32,33},{... | collective-permute-start | bytes 417800 | tf_op jit(solution)/shard_map/ppermute | solution.py:22
Sparse Core Ops, SparseCore 0:
  15.7 62.7 all-reduce.2
  108.7 41.8 all-reduce.4
